TPU v7x, 512 devices: a whole 4x8x8 slice. The times are simulated.
512 devices in a mesh: row: 32 (over y, x), layer: 16 (over z, core).
Axes of the slice: x: 4, y: 8, z: 8, core: 2. Of those that a mesh axis runs over, the one named last changes fastest.
Arguments:
- panel_left: bfloat16 [32, 32, 2048, 128], P('row', 'layer'), may hold values from -6 to 6
- panel_right: bfloat16 [32, 32, 2048, 128], P('row', 'layer'), may hold values from -0.125 to 0.125
- test_matrix: bfloat16 [2048, 128], replicated, may hold values from -6 to 6
- ranks: int32 [32, 32], P('row', 'layer'), may hold values from 32 to 128, as said below
- offsets: int32 [32, 2], P('row'), may hold values from 1 to 4, as said below
Outputs:
- basis: float32 [32, 2048, 2, 128], P('row', 'layer')
- update_right: float32 [32, 2048, 2, 128], P('row', 'layer')
Inputs may be any that keep to these rules, and one draw needn't show every extreme that they name: `ranks`: some tile has rank 128 and some tile has rank 128 // 4. An owner's 2 offsets differ from each other; the values 1 and 4 occur in every draw.
All inputs are finite; a program needn't handle non-finite values.
Results may differ from a plain program's by a relative error of at most 0.0003.
Values may be sent and summed in bfloat16 or wider, within the bound.
A program may use at most 64 MiB of HBM per device.

v0:
```python
import jax
import jax.numpy as jnp
from jax import lax
from jax.sharding import PartitionSpec as P

FRONTS = 4
TARGETS = 2


def passed_along(x, axis, by):
    length = lax.axis_size(axis)
    return lax.ppermute(x, axis, [(i, (i + by) % length) for i in range(length)])


def constant_of(front_item):
    return lambda: front_item


def orthonormal(sketch_rows, gram_mat):
    factor = jnp.linalg.cholesky(gram_mat)
    by_cols = jnp.transpose(sketch_rows, (1, 2, 0))
    solved = lax.linalg.triangular_solve(factor, by_cols, left_side=True, lower=True)
    return jnp.transpose(solved, (2, 0, 1))


def gram_of(sketch_rows, tile_size):
    return (
        jnp.einsum("bsr,bsq->srq", sketch_rows, sketch_rows, precision=lax.Precision.HIGHEST)
        / tile_size
    )


def on_device(panel_left, panel_right, test_matrix, ranks, offsets):
    high = lax.Precision.HIGHEST
    tile_size = panel_left.shape[2]
    rank_cap = panel_left.shape[3]
    share_rows = tile_size // lax.axis_size("layer")
    columns = lax.broadcasted_iota(jnp.int32, (ranks.shape[1], 1, rank_cap), 2)
    live_cols = (columns < ranks[0][:, None, None]).astype(jnp.bfloat16)
    own_left = panel_left[0] * live_cols
    own_right = panel_right[0] * live_cols
    stacked = jnp.stack([own_left, own_right])
    fronts = []
    moving = stacked
    for step_no in range(FRONTS):
        moving = passed_along(moving, "row", 1)
        fronts.append(moving)
    branches = [constant_of(front_item) for front_item in fronts]
    left_full = own_left.astype(jnp.float32)
    cores = []
    mixers = []
    partners = []
    for target in range(TARGETS):
        partner = lax.switch(offsets[0, target] - 1, branches)
        core_mat = jnp.einsum(
            "kbr,kbq->krq", own_right, partner[1], preferred_element_type=jnp.float32
        )
        probes = jnp.einsum(
            "kbr,bq->krq", partner[0], test_matrix, preferred_element_type=jnp.float32
        )
        mix_mat = jnp.einsum("krq,kqs->krs", core_mat, probes, precision=high)
        cores.append(core_mat)
        mixers.append(mix_mat)
        partners.append(partner[0].astype(jnp.float32))
    mixed = jnp.stack(mixers, axis=1)
    local_sketch = jnp.einsum("kbr,ksrq->bsq", left_full, mixed, precision=high)
    total_sketch = lax.psum(local_sketch, "layer")
    basis_all = orthonormal(total_sketch, gram_of(total_sketch, tile_size))
    first_own = lax.axis_index("layer") * share_rows
    basis_part = lax.dynamic_slice_in_dim(basis_all, first_own, share_rows, 0)
    reach = jnp.einsum("kbr,bsq->ksrq", left_full, basis_all, precision=high)
    weights = []
    for target in range(TARGETS):
        weight_mat = jnp.einsum("krq,krs->kqs", cores[target], reach[:, target], precision=high)
        weights.append(weight_mat)
    term_list = []
    for target in range(TARGETS):
        row_piece = lax.slice_in_dim(
            partners[target], 0, share_rows * lax.axis_size("layer"), axis=1
        )
        term_list.append(jnp.einsum("kbq,kqs->bs", row_piece, weights[target], precision=high))
    update_right = lax.psum_scatter(
        jnp.stack(term_list, axis=1) / tile_size, "layer", scatter_dimension=0, tiled=True
    )
    return (basis_part[None], update_right[None])


def solution(mesh):
    return jax.shard_map(
        on_device,
        mesh=mesh,
        in_specs=(
            P("row", "layer", None, None),
            P("row", "layer", None, None),
            P(),
            P("row", "layer"),
            P("row", None),
        ),
        out_specs=(P("row", "layer", None, None), P("row", "layer", None, None)),
        check_vma=False,
    )
```

profile of v0, /device:TPU:2, one launch (start us, length us, event | category | flops | bytes accessed | tf_op | source)
XLA Modules:
  0.0 479.9 jit_solution(14630520279900826652)
XLA Ops:
  7.2 0.0 copy-start
  7.2 0.0 all-reduce.2.cloned.1.call-start
  7.2 0.8 compare_convert_fusion
  8.0 1.7 broadcast_multiply_fusion.1
  9.7 0.0 copy-start.10
  9.7 0.2 pad_maximum_fusion
  9.9 3.4 collective-permute-start
  13.3 45.9 %collective-permute-done = bf16[2,2,2048,128]{3,2,1,0:T(8,128)(2,1)S(1)} collective-permute-done((bf16[2,2,2048,128]{3,2,1,0:T(8,128)(2,1)S(1)}, bf16[2,2,2048,128]{3,2,1,0:T(8,128)(2,1)S(1)}, u32[]{:S(2)}, u32[]{:S(2)}) %collective-permute-start) | collective-permute-done | bytes 2097184 | tf_op jit(solution)/shard_map/ppermute | solution.py:12
  59.2 0.0 copy-start.5
  59.2 3.4 collective-permute-start.1
  62.6 44.0 %collective-permute-done.1 = bf16[2,2,2048,128]{3,2,1,0:T(8,128)(2,1)S(1)} collective-permute-done((bf16[2,2,2048,128]{3,2,1,0:T(8,128)(2,1)S(1)}, bf16[2,2,2048,128]{3,2,1,0:T(8,128)(2,1)S(1)}, u32[]{:S(2)}, u32[]{:S(2)}) %collective-permute-start.1) | collective-permute-done | bytes 2097184 | tf_op jit(solution)/shard_map/ppermute | solution.py:12
  106.6 4.4 collective-permute-start.2
  110.9 43.6 %collective-permute-done.2 = bf16[2,2,2048,128]{3,2,1,0:T(8,128)(2,1)} collective-permute-done((bf16[2,2,2048,128]{3,2,1,0:T(8,128)(2,1)S(1)}, bf16[2,2,2048,128]{3,2,1,0:T(8,128)(2,1)}, u32[]{:S(2)}, u32[]{:S(2)}) %collective-permute-start.2) | collective-permute-done | bytes 2097184 | tf_op jit(solution)/shard_map/ppermute | solution.py:12
  154.5 4.0 collective-permute-start.3
  158.5 0.0 copy-done.10
  158.5 0.6 fusion.27
  160.4 41.0 %collective-permute-done.3 = bf16[2,2,2048,128]{3,2,1,0:T(8,128)(2,1)} collective-permute-done((bf16[2,2,2048,128]{3,2,1,0:T(8,128)(2,1)}, bf16[2,2,2048,128]{3,2,1,0:T(8,128)(2,1)}, u32[]{:S(2)}, u32[]{:S(2)}) %collective-permute-start.3) | collective-permute-done | bytes 2097184 | tf_op jit(solution)/shard_map/ppermute | solution.py:12
  201.4 0.0 copy-done.5
  201.4 3.1 conditional.2
  201.4 3.1 copy.36
  204.5 2.0 fusion.8
  206.5 0.0 copy-start.8
  206.5 0.0 copy-start.6
  206.5 2.2 fusion.7
  208.7 0.0 copy-done
  208.7 0.0 copy-done.8
  208.7 0.0 copy-start.2
  208.8 0.5 fusion.11
  209.2 0.1 copy-done.6
  209.4 0.5 fusion.12
  209.9 0.3 convolution_bitcast_fusion.4
  210.1 0.3 convolution_bitcast_fusion.3
  210.4 0.0 copy-done.2
  210.4 2.3 convolution_bitcast_fusion
  212.7 0.0 all-reduce.2.cloned.1.call-update
  212.8 0.2 reduce-scatter.2.cloned.1.call-start
  213.0 138.5 %all-reduce.2.cloned.1.call-done = f32[2048,2,128]{2,0,1:T(8,128)} async-done(((f32[2048,2,128]{2,0,1:T(8,128)}), f32[2048,2,128]{2,0,1:T(8,128)}) %all-reduce.2.cloned.1.call-update) | async-done | bytes 2097168 | tf_op jit(solution)/shard_map/psum | solution.py:67
  351.6 5.8 %fusion.28 = f32[2,128,128]{2,1,0:T(8,128)S(1)} fusion(f32[2048,2,128]{2,0,1:T(8,128)} %all-reduce.2.cloned.1.call-done), kind=kOutput, calls=%fused_computation.51 | convolution fusion | flops 805306368 | bytes 2228224 | tf_op jit(solution)/shard_map/bsr,bsq->srq/dot_general | solution.py:28
  357.4 0.1 copy.18
  357.5 23.5 %custom-call.7 = f32[2,128,128]{2,1,0:T(8,128)S(1)} custom-call(f32[2,128,128]{2,1,0:T(8,128)S(1)} %fusion.25), custom_call_target="Cholesky" | custom-call | tf_op jit(solution)/shard_map/jit(cholesky)/cholesky | solution.py:20
  381.0 0.1 compare_reduce_fusion
  381.1 0.1 select_bitcast_fusion
  381.2 19.9 %custom-call.8 = f32[2,1,128,128]{2,3,1,0:T(8,128)S(1)} custom-call(f32[2,1,128,128]{3,2,1,0:T(8,128)S(1)} %select_bitcast_fusion), custom_call_target="InvertDiagBlocksLowerTriangular" | custom-call | tf_op jit(solution)/shard_map/triangular_solve | solution.py:22
  401.1 0.0 copy-done.1
  401.1 0.0 copy-start.3
  401.2 2.0 fusion.2
  403.1 0.0 copy-done.3
  403.1 0.0 copy-start.4
  403.1 0.0 copy-start.7
  403.1 1.2 fusion.4
  404.3 0.0 copy-start.9
  404.3 0.4 fusion.22
  404.7 0.4 fusion.23
  405.1 0.0 copy-done.4
  405.1 0.3 copy-done.7
  405.5 1.0 convolution_bitcast_fusion.1
  406.5 0.0 copy-done.9
  406.5 1.0 convolution_bitcast_fusion.2
  407.5 1.4 maximum_multiply_fusion
  409.0 0.0 reduce-scatter.2.cloned.1.call-update
  409.0 0.9 dynamic-slice_bitcast_fusion
  409.9 0.8 copy.21
  410.7 60.7 %reduce-scatter.2.cloned.1.call-done = f32[128,2,128]{2,0,1:T(8,128)} async-done(((f32[2048,2,128]{2,0,1:T(8,128)}), f32[128,2,128]{2,0,1:T(8,128)}) %reduce-scatter.2.cloned.1.call-update) | async-done | bytes 131088 | tf_op jit(solution)/shard_map/reduce_scatter | solution.py:82
  471.4 1.7 copy.22
  (6 shorter events, 0.1 us)
Async XLA Ops:
  7.2 201.6 %copy-start = (bf16[2048,128]{1,0:T(8,128)(2,1)S(1)}, bf16[2048,128]{1,0:T(8,128)(2,1)}, u32[]{:S(2)}) copy-start(bf16[2048,128]{1,0:T(8,128)(2,1)} %param.15) | copy-start | bytes 1572868
  7.2 344.4 %all-reduce.2.cloned.1.call-start = ((), (), s32[]{:S(2)}) async-start(), calls=%async_computation.1 | async-start | bytes 4194304 | tf_op jit(solution)/shard_map/psum | solution.py:67
  9.7 148.8 %copy-start.10 = (s32[1,2]{1,0:T(1,128)S(1)}, s32[1,2]{1,0:T(1,128)}, u32[]{:S(2)}) copy-start(s32[1,2]{1,0:T(1,128)} %param.17) | copy-start | bytes 28
  9.9 49.3 %collective-permute-start = (bf16[2,2,2048,128]{3,2,1,0:T(8,128)(2,1)S(1)}, bf16[2,2,2048,128]{3,2,1,0:T(8,128)(2,1)S(1)}, u32[]{:S(2)}, u32[]{:S(2)}) collective-permute-start(bf16[2,2,2048,128]{3,2,1,0:T(8,128)(2,1)S(1)} %pad_maximum_fusion), channel_id=1, source_target_pairs={{0,16},{16,32},{32,48},{48,64},{64,80},{80,96},{96,112},{112,128},... | collective-permute-start | bytes 6291464 | tf_op jit(solution)/shard_map/ppermute | solution.py:12
  59.2 142.2 %copy-start.5 = (bf16[2,2,2048,128]{3,2,1,0:T(8,128)(2,1)}, bf16[2,2,2048,128]{3,2,1,0:T(8,128)(2,1)S(1)}, u32[]{:S(2)}) copy-start(bf16[2,2,2048,128]{3,2,1,0:T(8,128)(2,1)S(1)} %collective-permute-done) | copy-start | bytes 6291460
  59.2 47.4 %collective-permute-start.1 = (bf16[2,2,2048,128]{3,2,1,0:T(8,128)(2,1)S(1)}, bf16[2,2,2048,128]{3,2,1,0:T(8,128)(2,1)S(1)}, u32[]{:S(2)}, u32[]{:S(2)}) collective-permute-start(bf16[2,2,2048,128]{3,2,1,0:T(8,128)(2,1)S(1)} %collective-permute-done), channel_id=1, source_target_pairs={{0,16},{16,32},{32,48},{48,64},{64,80},{80,96},{96,112},{112,128},... | collective-permute-start | bytes 6291464 | tf_op jit(solution)/shard_map/ppermute | solution.py:12
  106.6 48.0 %collective-permute-start.2 = (bf16[2,2,2048,128]{3,2,1,0:T(8,128)(2,1)S(1)}, bf16[2,2,2048,128]{3,2,1,0:T(8,128)(2,1)}, u32[]{:S(2)}, u32[]{:S(2)}) collective-permute-start(bf16[2,2,2048,128]{3,2,1,0:T(8,128)(2,1)S(1)} %collective-permute-done.1), channel_id=1, source_target_pairs={{0,16},{16,32},{32,48},{48,64},{64,80},{80,96},{96,112},{112,128},... | collective-permute-start | bytes 6291464 | tf_op jit(solution)/shard_map/ppermute | solution.py:12
  154.5 46.9 %collective-permute-start.3 = (bf16[2,2,2048,128]{3,2,1,0:T(8,128)(2,1)}, bf16[2,2,2048,128]{3,2,1,0:T(8,128)(2,1)}, u32[]{:S(2)}, u32[]{:S(2)}) collective-permute-start(bf16[2,2,2048,128]{3,2,1,0:T(8,128)(2,1)} %collective-permute-done.2), channel_id=1, source_target_pairs={{0,16},{16,32},{32,48},{48,64},{64,80},{80,96},{96,112},{112,128},... | collective-permute-start | bytes 6291464 | tf_op jit(solution)/shard_map/ppermute | solution.py:12
  206.5 2.2 copy-start.8
  206.5 2.8 copy-start.6
  208.7 1.7 copy-start.2
  212.8 258.6 %reduce-scatter.2.cloned.1.call-start = ((), (), s32[]{:S(2)}) async-start(), calls=%async_computation.2 | async-start | bytes 2228224 | tf_op jit(solution)/shard_map/reduce_scatter | solution.py:82
  351.6 49.6 %copy-start.1 = (f32[2048,2,128]{2,0,1:T(8,128)S(1)}, f32[2048,2,128]{2,0,1:T(8,128)}, u32[]{:S(2)}) copy-start(f32[2048,2,128]{2,0,1:T(8,128)} %all-reduce.2.cloned.1.call-done) | copy-start | bytes 6291460
  401.1 2.0 copy-start.3
  403.1 2.0 copy-start.4
  403.1 2.3 copy-start.7
  404.3 2.2 copy-start.9
Sparse Core Ops, SparseCore 0:
  212.9 138.6 all-reduce.1
  409.1 62.2 reduce-scatter.1
where the time goes:
time: 480 us
  waiting for transfers between devices  374 us (78%)
  other arithmetic  47.7 us (10%)
  matrix products  19.8 us (4%)
  between operations  15.7 us (3%)
  starting transfers between devices  15.4 us (3%)
  local copies, waits for them, and re-layouts  7.61 us (2%)
    ppermute x4, waiting for transfers between devices, passed_along(): lax.ppermute(x, axis, [(i, (i + by) % length) for i in range(length)])  174 us
    psum x1, waiting for transfers between devices, on_device(): total_sketch = lax.psum(local_sketch, 'layer')  139 us
    reduce_scatter x1, waiting for transfers between devices, on_device(): lax.psum_scatter(jnp.stack(term_list, axis=1) / tile_size, 'layer', scatt...  60.7 us
    another operation x4, other arithmetic, orthonormal(): factor = jnp.linalg.cholesky(gram_mat)  23.6 us
    another operation x3, other arithmetic, orthonormal(): lax.linalg.triangular_solve(factor, by_cols, left_side=True, lower=True)  20 us
    ppermute x4, starting transfers between devices, passed_along(): lax.ppermute(x, axis, [(i, (i + by) % length) for i in range(length)])  15.1 us
  transfers between devices with their start and end apart: 6, of which 6 were waited for; matrix products, arithmetic and copies ran while one was open for 0% of the time, Pallas kernels for 0%

commit v1 on v0

--- a/solution.py
+++ b/solution.py
@@ -5,6 +5,14 @@
 
 FRONTS = 4
 TARGETS = 2
+
+
+def add_in_pairs(x, mesh_axis):
+    size, total = (lax.axis_size(mesh_axis), x)
+    for far in [1 << k for k in range(size.bit_length() - 1)]:
+        route = [(i, i ^ far) for i in range(size)]
+        total = total + lax.ppermute(total, mesh_axis, route)
+    return total
 
 
 def passed_along(x, axis, by):
@@ -64,7 +72,7 @@
         partners.append(partner[0].astype(jnp.float32))
     mixed = jnp.stack(mixers, axis=1)
     local_sketch = jnp.einsum("kbr,ksrq->bsq", left_full, mixed, precision=high)
-    total_sketch = lax.psum(local_sketch, "layer")
+    total_sketch = add_in_pairs(local_sketch, "layer")
     basis_all = orthonormal(total_sketch, gram_of(total_sketch, tile_size))
     first_own = lax.axis_index("layer") * share_rows
     basis_part = lax.dynamic_slice_in_dim(basis_all, first_own, share_rows, 0)

time: 480 us -> 606 us (1.26)
  the two profiles are of different devices: /device:TPU:2 before, /device:TPU:4 now
where the time goes in v1:
time: 606 us
  waiting for transfers between devices  473 us (78%)
  other arithmetic  48.4 us (8%)
  starting transfers between devices  41.8 us (7%)
  matrix products  17.9 us (3%)
  between operations  15.7 us (3%)
  local copies, waits for them, and re-layouts  8.6 us (1%)
    ppermute x4, waiting for transfers between devices, add_in_pairs(): total = total + lax.ppermute(total, mesh_axis, route)  231 us
    ppermute x4, waiting for transfers between devices, passed_along(): lax.ppermute(x, axis, [(i, (i + by) % length) for i in range(length)])  175 us
    reduce_scatter x1, waiting for transfers between devices, on_device(): lax.psum_scatter(jnp.stack(term_list, axis=1) / tile_size, 'layer', scatt...  67.5 us
    ppermute x4, starting transfers between devices, add_in_pairs(): total = total + lax.ppermute(total, mesh_axis, route)  25.1 us
    another operation x4, other arithmetic, orthonormal(): factor = jnp.linalg.cholesky(gram_mat)  23.6 us
    another operation x3, other arithmetic, orthonormal(): lax.linalg.triangular_solve(factor, by_cols, left_side=True, lower=True)  20 us
    ppermute x4, starting transfers between devices, passed_along(): lax.ppermute(x, axis, [(i, (i + by) % length) for i in range(length)])  16.6 us
  transfers between devices with their start and end apart: 9, of which 9 were waited for; matrix products, arithmetic and copies ran while one was open for 0% of the time, Pallas kernels for 0%

profile of v1, /device:TPU:4, one launch (start us, length us, event | category | flops | bytes accessed | tf_op | source)
XLA Modules:
  0.0 605.8 jit_solution(15716613199220405674)
XLA Ops:
  7.2 0.0 copy-start
  7.2 0.0 reduce-scatter.2.cloned.1.call-start
  7.2 0.8 compare_convert_fusion
  8.0 1.7 broadcast_multiply_fusion.1
  9.7 0.0 copy-start.10
  9.7 0.2 pad_maximum_fusion
  9.9 3.1 collective-permute-start
  13.0 46.1 %collective-permute-done = bf16[2,2,2048,128]{3,2,1,0:T(8,128)(2,1)S(1)} collective-permute-done((bf16[2,2,2048,128]{3,2,1,0:T(8,128)(2,1)S(1)}, bf16[2,2,2048,128]{3,2,1,0:T(8,128)(2,1)S(1)}, u32[]{:S(2)}, u32[]{:S(2)}) %collective-permute-start) | collective-permute-done | bytes 2097184 | tf_op jit(solution)/shard_map/ppermute | solution.py:20
  59.2 3.1 collective-permute-start.1
  62.3 45.3 %collective-permute-done.1 = bf16[2,2,2048,128]{3,2,1,0:T(8,128)(2,1)S(1)} collective-permute-done((bf16[2,2,2048,128]{3,2,1,0:T(8,128)(2,1)S(1)}, bf16[2,2,2048,128]{3,2,1,0:T(8,128)(2,1)S(1)}, u32[]{:S(2)}, u32[]{:S(2)}) %collective-permute-start.1) | collective-permute-done | bytes 2097184 | tf_op jit(solution)/shard_map/ppermute | solution.py:20
  107.5 4.2 collective-permute-start.2
  111.8 43.3 %collective-permute-done.2 = bf16[2,2,2048,128]{3,2,1,0:T(8,128)(2,1)} collective-permute-done((bf16[2,2,2048,128]{3,2,1,0:T(8,128)(2,1)S(1)}, bf16[2,2,2048,128]{3,2,1,0:T(8,128)(2,1)}, u32[]{:S(2)}, u32[]{:S(2)}) %collective-permute-start.2) | collective-permute-done | bytes 2097184 | tf_op jit(solution)/shard_map/ppermute | solution.py:20
  155.1 6.2 %collective-permute-start.3 = (bf16[2,2,2048,128]{3,2,1,0:T(8,128)(2,1)}, bf16[2,2,2048,128]{3,2,1,0:T(8,128)(2,1)}, u32[]{:S(2)}, u32[]{:S(2)}) collective-permute-start(bf16[2,2,2048,128]{3,2,1,0:T(8,128)(2,1)} %collective-permute-done.2), channel_id=1, source_target_pairs={{0,16},{16,32},{32,48},{48,64},{64,80},{80,96},{96,112},{112,128},... | collective-permute-start | bytes 6291464 | tf_op jit(solution)/shard_map/ppermute | solution.py:20
  161.3 0.0 copy-done.10
  161.3 0.6 fusion.30
  163.2 40.6 %collective-permute-done.3 = bf16[2,2,2048,128]{3,2,1,0:T(8,128)(2,1)} collective-permute-done((bf16[2,2,2048,128]{3,2,1,0:T(8,128)(2,1)}, bf16[2,2,2048,128]{3,2,1,0:T(8,128)(2,1)}, u32[]{:S(2)}, u32[]{:S(2)}) %collective-permute-start.3) | collective-permute-done | bytes 2097184 | tf_op jit(solution)/shard_map/ppermute | solution.py:20
  203.8 0.0 copy-done.5
  203.8 1.4 conditional.2
  203.8 1.4 copy.34
  205.2 2.0 fusion.8
  207.2 1.4 conditional.3
  207.2 1.4 copy.31
  208.6 2.2 fusion.7
  210.8 0.0 copy-done.8
  210.8 0.5 fusion.11
  211.3 0.1 copy-done.6
  211.4 0.5 fusion.12
  211.9 0.3 convolution_bitcast_fusion.4
  212.2 0.3 convolution_bitcast_fusion.3
  212.5 1.0 convolution_bitcast_fusion
  213.5 1.9 collective-permute-start.4
  215.4 4.1 collective-permute-done.4
  219.5 0.2 add.31
  219.8 8.5 %collective-permute-start.5 = (f32[2048,2,128]{2,0,1:T(8,128)S(1)}, f32[2048,2,128]{2,0,1:T(8,128)S(1)}, u32[]{:S(2)}, u32[]{:S(2)}) collective-permute-start(f32[2048,2,128]{2,0,1:T(8,128)S(1)} %add.31), channel_id=1, source_target_pairs={{0,2},{1,3},{2,0},{3,1},{4,6},{5,7},{6,4},{7,5},{8,10},{9,11},{10,... | collective-permute-start | bytes 6291464 | tf_op jit(solution)/shard_map/ppermute | solution.py:14
  228.3 45.9 %collective-permute-done.5 = f32[2048,2,128]{2,0,1:T(8,128)S(1)} collective-permute-done((f32[2048,2,128]{2,0,1:T(8,128)S(1)}, f32[2048,2,128]{2,0,1:T(8,128)S(1)}, u32[]{:S(2)}, u32[]{:S(2)}) %collective-permute-start.5) | collective-permute-done | bytes 2097184 | tf_op jit(solution)/shard_map/ppermute | solution.py:14
  274.2 0.2 add.32
  274.4 6.1 %collective-permute-start.6 = (f32[2048,2,128]{2,0,1:T(8,128)S(1)}, f32[2048,2,128]{2,0,1:T(8,128)S(1)}, u32[]{:S(2)}, u32[]{:S(2)}) collective-permute-start(f32[2048,2,128]{2,0,1:T(8,128)S(1)} %add.32), channel_id=1, source_target_pairs={{0,4},{1,5},{2,6},{3,7},{4,0},{5,1},{6,2},{7,3},{8,12},{9,13},{10,... | collective-permute-start | bytes 6291464 | tf_op jit(solution)/shard_map/ppermute | solution.py:14
  280.5 90.3 %collective-permute-done.6 = f32[2048,2,128]{2,0,1:T(8,128)S(1)} collective-permute-done((f32[2048,2,128]{2,0,1:T(8,128)S(1)}, f32[2048,2,128]{2,0,1:T(8,128)S(1)}, u32[]{:S(2)}, u32[]{:S(2)}) %collective-permute-start.6) | collective-permute-done | bytes 2097184 | tf_op jit(solution)/shard_map/ppermute | solution.py:14
  370.9 0.2 add.33
  371.1 8.6 %collective-permute-start.7 = (f32[2048,2,128]{2,0,1:T(8,128)S(1)}, f32[2048,2,128]{2,0,1:T(8,128)S(1)}, u32[]{:S(2)}, u32[]{:S(2)}) collective-permute-start(f32[2048,2,128]{2,0,1:T(8,128)S(1)} %add.33), channel_id=1, source_target_pairs={{0,8},{1,9},{2,10},{3,11},{4,12},{5,13},{6,14},{7,15},{8,0},{9,1},... | collective-permute-start | bytes 6291464 | tf_op jit(solution)/shard_map/ppermute | solution.py:14
  379.7 90.1 %collective-permute-done.7 = f32[2048,2,128]{2,0,1:T(8,128)S(1)} collective-permute-done((f32[2048,2,128]{2,0,1:T(8,128)S(1)}, f32[2048,2,128]{2,0,1:T(8,128)S(1)}, u32[]{:S(2)}, u32[]{:S(2)}) %collective-permute-start.7) | collective-permute-done | bytes 2097184 | tf_op jit(solution)/shard_map/ppermute | solution.py:14
  469.9 1.3 copy-done.4
  471.2 3.6 fusion.14
  474.8 0.1 copy.18
  474.9 23.5 %custom-call.7 = f32[2,128,128]{2,1,0:T(8,128)S(1)} custom-call(f32[2,128,128]{2,1,0:T(8,128)S(1)} %fusion.28), custom_call_target="Cholesky" | custom-call | tf_op jit(solution)/shard_map/jit(cholesky)/cholesky | solution.py:28
  498.4 0.1 compare_reduce_fusion
  498.5 0.1 select_bitcast_fusion
  498.6 19.9 %custom-call.8 = f32[2,1,128,128]{2,3,1,0:T(8,128)S(1)} custom-call(f32[2,1,128,128]{3,2,1,0:T(8,128)S(1)} %select_bitcast_fusion), custom_call_target="InvertDiagBlocksLowerTriangular" | custom-call | tf_op jit(solution)/shard_map/triangular_solve | solution.py:30
  518.5 0.0 copy-start.2
  518.5 3.7 fusion.2
  522.2 0.0 copy-done.2
  522.2 0.0 copy-start.3
  522.2 1.2 fusion.4
  523.4 0.4 fusion.25
  523.8 0.4 fusion.26
  524.3 0.3 copy-done.7
  524.6 1.0 convolution_bitcast_fusion.1
  525.6 1.0 convolution_bitcast_fusion.2
  526.6 1.5 maximum_multiply_fusion
  528.1 0.0 reduce-scatter.2.cloned.1.call-update
  528.1 0.9 dynamic-slice_bitcast_fusion
  529.0 0.8 copy.21
  529.8 67.5 %reduce-scatter.2.cloned.1.call-done = f32[128,2,128]{2,0,1:T(8,128)} async-done(((f32[2048,2,128]{2,0,1:T(8,128)}), f32[128,2,128]{2,0,1:T(8,128)}) %reduce-scatter.2.cloned.1.call-update) | async-done | bytes 131088 | tf_op jit(solution)/shard_map/reduce_scatter | solution.py:90
  597.3 1.7 copy.22
  (15 shorter events, 0.1 us)
Async XLA Ops:
  7.2 203.6 %copy-start = (bf16[2048,128]{1,0:T(8,128)(2,1)S(1)}, bf16[2048,128]{1,0:T(8,128)(2,1)}, u32[]{:S(2)}) copy-start(bf16[2048,128]{1,0:T(8,128)(2,1)} %param.15) | copy-start | bytes 1572868
  7.2 590.1 %reduce-scatter.2.cloned.1.call-start = ((), (), s32[]{:S(2)}) async-start(), calls=%async_computation.1 | async-start | bytes 2228224 | tf_op jit(solution)/shard_map/reduce_scatter | solution.py:90
  9.7 151.7 %copy-start.10 = (s32[1,2]{1,0:T(1,128)S(1)}, s32[1,2]{1,0:T(1,128)}, u32[]{:S(2)}) copy-start(s32[1,2]{1,0:T(1,128)} %param.17) | copy-start | bytes 28
  9.9 49.3 %collective-permute-start = (bf16[2,2,2048,128]{3,2,1,0:T(8,128)(2,1)S(1)}, bf16[2,2,2048,128]{3,2,1,0:T(8,128)(2,1)S(1)}, u32[]{:S(2)}, u32[]{:S(2)}) collective-permute-start(bf16[2,2,2048,128]{3,2,1,0:T(8,128)(2,1)S(1)} %pad_maximum_fusion), channel_id=1, source_target_pairs={{0,16},{16,32},{32,48},{48,64},{64,80},{80,96},{96,112},{112,128},... | collective-permute-start | bytes 6291464 | tf_op jit(solution)/shard_map/ppermute | solution.py:20
  59.2 144.6 %copy-start.5 = (bf16[2,2,2048,128]{3,2,1,0:T(8,128)(2,1)}, bf16[2,2,2048,128]{3,2,1,0:T(8,128)(2,1)S(1)}, u32[]{:S(2)}) copy-start(bf16[2,2,2048,128]{3,2,1,0:T(8,128)(2,1)S(1)} %collective-permute-done) | copy-start | bytes 6291460
  59.2 48.4 %collective-permute-start.1 = (bf16[2,2,2048,128]{3,2,1,0:T(8,128)(2,1)S(1)}, bf16[2,2,2048,128]{3,2,1,0:T(8,128)(2,1)S(1)}, u32[]{:S(2)}, u32[]{:S(2)}) collective-permute-start(bf16[2,2,2048,128]{3,2,1,0:T(8,128)(2,1)S(1)} %collective-permute-done), channel_id=1, source_target_pairs={{0,16},{16,32},{32,48},{48,64},{64,80},{80,96},{96,112},{112,128},... | collective-permute-start | bytes 6291464 | tf_op jit(solution)/shard_map/ppermute | solution.py:20
  107.5 47.6 %collective-permute-start.2 = (bf16[2,2,2048,128]{3,2,1,0:T(8,128)(2,1)S(1)}, bf16[2,2,2048,128]{3,2,1,0:T(8,128)(2,1)}, u32[]{:S(2)}, u32[]{:S(2)}) collective-permute-start(bf16[2,2,2048,128]{3,2,1,0:T(8,128)(2,1)S(1)} %collective-permute-done.1), channel_id=1, source_target_pairs={{0,16},{16,32},{32,48},{48,64},{64,80},{80,96},{96,112},{112,128},... | collective-permute-start | bytes 6291464 | tf_op jit(solution)/shard_map/ppermute | solution.py:20
  155.1 48.7 %collective-permute-start.3 = (bf16[2,2,2048,128]{3,2,1,0:T(8,128)(2,1)}, bf16[2,2,2048,128]{3,2,1,0:T(8,128)(2,1)}, u32[]{:S(2)}, u32[]{:S(2)}) collective-permute-start(bf16[2,2,2048,128]{3,2,1,0:T(8,128)(2,1)} %collective-permute-done.2), channel_id=1, source_target_pairs={{0,16},{16,32},{32,48},{48,64},{64,80},{80,96},{96,112},{112,128},... | collective-permute-start | bytes 6291464 | tf_op jit(solution)/shard_map/ppermute | solution.py:20
  208.6 2.2 copy-start.8
  208.6 2.9 copy-start.6
  210.8 1.7 copy-start.1
  213.5 6.1 collective-permute-start.4
  219.8 54.5 %collective-permute-start.5 = (f32[2048,2,128]{2,0,1:T(8,128)S(1)}, f32[2048,2,128]{2,0,1:T(8,128)S(1)}, u32[]{:S(2)}, u32[]{:S(2)}) collective-permute-start(f32[2048,2,128]{2,0,1:T(8,128)S(1)} %add.31), channel_id=1, source_target_pairs={{0,2},{1,3},{2,0},{3,1},{4,6},{5,7},{6,4},{7,5},{8,10},{9,11},{10,... | collective-permute-start | bytes 6291464 | tf_op jit(solution)/shard_map/ppermute | solution.py:14
  274.4 96.4 %collective-permute-start.6 = (f32[2048,2,128]{2,0,1:T(8,128)S(1)}, f32[2048,2,128]{2,0,1:T(8,128)S(1)}, u32[]{:S(2)}, u32[]{:S(2)}) collective-permute-start(f32[2048,2,128]{2,0,1:T(8,128)S(1)} %add.32), channel_id=1, source_target_pairs={{0,4},{1,5},{2,6},{3,7},{4,0},{5,1},{6,2},{7,3},{8,12},{9,13},{10,... | collective-permute-start | bytes 6291464 | tf_op jit(solution)/shard_map/ppermute | solution.py:14
  371.1 98.8 %collective-permute-start.7 = (f32[2048,2,128]{2,0,1:T(8,128)S(1)}, f32[2048,2,128]{2,0,1:T(8,128)S(1)}, u32[]{:S(2)}, u32[]{:S(2)}) collective-permute-start(f32[2048,2,128]{2,0,1:T(8,128)S(1)} %add.33), channel_id=1, source_target_pairs={{0,8},{1,9},{2,10},{3,11},{4,12},{5,13},{6,14},{7,15},{8,0},{9,1},... | collective-permute-start | bytes 6291464 | tf_op jit(solution)/shard_map/ppermute | solution.py:14
  469.9 1.3 copy-start.4
  518.5 3.7 copy-start.2
  522.2 2.0 copy-start.3
  522.2 2.3 copy-start.7
  523.4 2.2 copy-start.9
Sparse Core Ops, SparseCore 0:
  528.2 68.9 reduce-scatter.1
